TPU v7x, 32 devices: a whole 2x2x4 slice. The times are simulated.
32 devices in a mesh: groups: 2 (over y), seq: 8 (over z, x), section: 2 (over core).
Axes of the slice: x: 2, y: 2, z: 4, core: 2. Of those that a mesh axis runs over, the one named last changes fastest.
Arguments:
- prompt: bfloat16 [4096, 4096], P(('groups', 'seq'), 'section'), parts along dimension 0, may hold values from -6 to 6
- in_gain: float32 [2, 4096], P(None, 'section'), may hold values from 0.5 to 1.5
- conv_w: bfloat16 [2, 4, 4096], P(None, None, 'section'), may hold values from -3 to 3
- a_log: float32 [2, 64], P(None, 'section'), may hold values from -16 to -2
- out_gain: float32 [2, 4096], P(None, 'section'), may hold values from 0.5 to 1.5
- dt_raw: float32 [2, 4096, 64], P(None, ('groups', 'seq'), 'section'), parts along dimension 1, may hold values from -2.5 to 1.5
- proj: bfloat16 [2, 4096, 2, 256], P(None, ('groups', 'seq'), None, 'section'), parts along dimension 1, may hold values from -6 to 6
Outputs:
- streams: bfloat16 [2, 4096, 4096], P(None, ('groups', 'seq'), 'section'), parts along dimension 1
There are 2 independent parts, one for each index of `groups`. A program takes and returns all parts, laid end to end along the dimension named above; an argument that names none is the same for every part. Nothing has to cross between parts.
All inputs are finite; a program needn't handle non-finite values.
Results may differ from a plain program's by a relative error of at most 0.0064.
Values may be sent and summed in bfloat16 or wider, within the bound.
A program may use at most 256 MiB of HBM per device.

v0:
```python
import jax
import jax.numpy as jnp
from jax import lax
from jax.sharding import PartitionSpec as P

D = 4096
STATE = 64
LAYERS = 2


EPSILON = 1e-05


def from_behind(block, axis, distance):
    devices = range(lax.axis_size(axis))
    route = [(i - distance, i) for i in devices if i - distance in devices]
    return lax.ppermute(block, axis, route)


def carried_in(value, axis, join, neutral):
    count, mine = (lax.axis_size(axis), lax.axis_index(axis))
    pieces = jax.tree.map(lambda part: lax.all_gather(part, axis), value)
    total = jax.tree.map(
        lambda part, zero: jnp.full_like(part, 0) + jnp.asarray(zero, part.dtype), value, neutral
    )

    def hop(position, total):
        longer = join(total, jax.tree.map(lambda part: part[position], pieces))
        return jax.tree.map(lambda new, old: jnp.where(position < mine, new, old), longer, total)

    return lax.fori_loop(0, count - 1, hop, total)


def combine_states(earlier, later):
    return (earlier[0] * later[0], later[0][:, None, None] * earlier[1] + later[1])


def group_terms(pieces):
    mixed_g, b_g, c_g, delta_g, decay_g = pieces
    length = mixed_g.shape[0]
    running = jnp.cumsum(decay_g, axis=0)
    scores = jnp.einsum("tn,sn->ts", c_g, b_g, preferred_element_type=jnp.float32)
    lower = jnp.arange(length)[:, None] >= jnp.arange(length)[None, :]
    gap = running.T[:, :, None] - running.T[:, None, :]
    decay = jnp.where(lower[None], jnp.exp(jnp.where(lower[None], gap, 0.0)), 0.0)
    weights = (decay * delta_g.T[:, None, :] * scores[None]).astype(jnp.bfloat16)
    intra = jnp.einsum("hts,shp->thp", weights, mixed_g, preferred_element_type=jnp.float32)
    scaled = (jnp.exp(running[-1][None, :] - running) * delta_g)[:, :, None] * mixed_g.astype(
        jnp.float32
    )
    scaled = scaled.astype(jnp.bfloat16)
    local_state = jnp.einsum("thp,tn->hpn", scaled, b_g, preferred_element_type=jnp.float32)
    return (running, intra, local_state)


def local(prompt, in_gain, conv_w, a_log, out_gain, dt_raw, proj):
    stream = prompt
    tile_rows, width_d = stream.shape
    heads = a_log.shape[1]
    head_dim = width_d // heads
    groups_here = proj.shape[3] // STATE
    per_group = heads // groups_here
    taps = conv_w.shape[1]
    results = []
    for layer in range(LAYERS):
        gain_in = in_gain[layer]
        widened = stream.astype(jnp.float32)
        squares = jnp.sum(widened * widened, axis=1)
        row_total = lax.psum(squares, "section")
        normed = (widened * lax.rsqrt(row_total / D + EPSILON)[:, None] * gain_in).astype(
            jnp.bfloat16
        )
        received = from_behind(normed[tile_rows - (taps - 1) :], "seq", 1)
        padded = jnp.concatenate([received, normed], axis=0)
        tap_weights = conv_w[layer].astype(jnp.float32)
        total = jnp.zeros((tile_rows, width_d), jnp.float32)
        for offset in range(taps):
            total = total + tap_weights[offset] * padded[offset : offset + tile_rows].astype(
                jnp.float32
            )
        mixed = jax.nn.silu(total).astype(jnp.bfloat16)
        delta = jax.nn.softplus(dt_raw[layer])
        log_decay = -delta * jnp.exp(a_log[layer])
        b_groups = proj[layer][:, 0].reshape(tile_rows, groups_here, STATE)
        c_groups = proj[layer][:, 1].reshape(tile_rows, groups_here, STATE)
        stacked = (
            mixed.reshape(tile_rows, groups_here, per_group, head_dim).transpose(1, 0, 2, 3),
            b_groups.transpose(1, 0, 2),
            c_groups.transpose(1, 0, 2),
            delta.reshape(tile_rows, groups_here, per_group).transpose(1, 0, 2),
            log_decay.reshape(tile_rows, groups_here, per_group).transpose(1, 0, 2),
        )
        running_g, intra_g, local_g = lax.map(group_terms, stacked)
        running = running_g.transpose(1, 0, 2).reshape(tile_rows, heads)
        intra = intra_g.transpose(1, 0, 2, 3).reshape(tile_rows, heads, head_dim)
        local_state = local_g.reshape(heads, head_dim, STATE)
        decay_all = jnp.exp(running[-1])
        before_decay, entering = carried_in(
            (decay_all, local_state),
            "seq",
            combine_states,
            (jnp.ones_like(decay_all), jnp.zeros_like(local_state)),
        )
        c_heads = jnp.repeat(c_groups, per_group, axis=1).astype(jnp.float32)
        inter = jnp.exp(running)[:, :, None] * jnp.einsum(
            "thn,hpn->thp", c_heads, entering, precision=lax.Precision.HIGHEST
        )
        combined = intra + inter
        normed_out = (
            combined * lax.rsqrt(jnp.mean(combined * combined, axis=-1, keepdims=True) + EPSILON)
        ).reshape(tile_rows, width_d)
        stream = (widened + normed_out * out_gain[layer]).astype(jnp.bfloat16)
        results.append(stream)
    return jnp.stack(results)


def solution(mesh):
    in_specs = (
        P(("groups", "seq"), "section"),
        P(None, "section"),
        P(None, None, "section"),
        P(None, "section"),
        P(None, "section"),
        P(None, ("groups", "seq"), "section"),
        P(None, ("groups", "seq"), None, "section"),
    )
    out_specs = P(None, ("groups", "seq"), "section")
    return jax.shard_map(local, mesh=mesh, in_specs=in_specs, out_specs=out_specs, check_vma=False)
```

profile of v0, /device:TPU:24, one launch (start us, length us, event | category | flops | bytes accessed | tf_op | source)
XLA Modules:
  0.0 369.0 jit_solution(9108921778933378324)
XLA Ops:
  8.4 2.5 psum.14
  11.4 3.4 collective-permute-start
  18.0 10.3 %collective-permute-done = bf16[3,2048]{0,1:T(8,128)(2,1)} collective-permute-done((bf16[3,2048]{0,1:T(8,128)(2,1)S(1)}, bf16[3,2048]{0,1:T(8,128)(2,1)}, u32[]{:S(2)}, u32[]{:S(2)}) %collective-permute-start) | collective-permute-done | bytes 12320 | tf_op jit(solution)/shard_map/ppermute | solution.py:17
  28.3 4.3 %multiply_convert_fusion.15 = bf16[256,2048]{0,1:T(8,128)(2,1)S(1)} fusion(bf16[256,2048]{0,1:T(8,128)(2,1)S(1)} %fusion.60, bf16[3,2048]{0,1:T(8,128)(2,1)} %collective-permute-done, f32[2048]{0:T(1024)S(1)} %bitcast.332, f32[2048]{0:T(1024)S(1)} %bitcast.331, f32[2048]{0:T(1024)S(1)} %bitcast.330, f32[2048]{0:T(1024)S(1)} %bitcast.333), kind=kLoop, calls=%fused_computation.110 | loop fusion | flops 13107200 | bytes 2142208 | tf_op jit(solution)/shard_map/convert_element_type | solution.py:81
  32.6 1.6 broadcast.92.clone
  34.9 9.6 %while.56 = (s32[]{:T(128)}, f32[2,256,16]{1,2,0:T(8,128)}, f32[2,256,16,64]{1,3,2,0:T(8,128)}, f32[2,16,64,64]{3,2,1,0:T(8,128)S(1)}, f32[2,256,16]{1,2,0:T(8,1...) while((s32[]{:T(128)}, f32[2,256,16]{1,2,0:T(8,128)}, ...), condition=%wide.region_5.6_spmd, body=%wide.region_2.5_spmd.sunk | while | flops 183844912 | bytes 3675649 | solution.py:93
  36.0 2.4 fusion.114
  40.8 2.4 fusion.114
  47.7 15.3 %all-gather = f32[8,1,32]{2,1,0:T(1,128)S(1)} all-gather(f32[1,1,32]{2,1,0:T(1,128)S(1)} %reshape.222), channel_id=1, replica_groups=mesh['groups'=2,'seq'=8,'section'=2] {'seq'}, dimensions={0}, use_global_device_ids=true | all-gather | bytes 1152 | tf_op jit(solution)/shard_map/all_gather | solution.py:22
  63.7 105.1 %all-gather.5.cloned.1.call-done = f32[8,32,64,64]{3,2,1,0:T(8,128)} async-done(((f32[1,32,64,64]{3,2,1,0:T(8,128)}), f32[8,32,64,64]{3,2,1,0:T(8,128)}) %all-gather.5.cloned.1.call-update) | async-done | bytes 4194320 | tf_op jit(solution)/shard_map/all_gather | solution.py:22
  168.8 10.5 %while.58 = (s32[]{:T(128)}, f32[32,64,64]{2,1,0:T(8,128)S(1)}, s32[]{:T(128)}, f32[8,32]{1,0:T(8,128)S(1)}, f32[8,32,64,64]{3,2,1,0:T(8,128)}, /*index=5*/s32[]{:T(128)}, s32[]{:T(128)}) while((s32[]{:T(128)}, f32[32,64,64]{2,1,0:T(8,128)S(1)}, s32[]{:T(128)}, f32[8,32]{1,0:T(8,128)S(1)}, f32[8,32,64,64]{3,2,1,0:T(8,128)}, ...), condition=%wide.region_7.8_spmd.clone, body=%wide.region_6.7_spmd.clone.sunk | while | flops 524292 | bytes 1573353 | solution.py:31
  179.4 2.9 multiply_reduce_fusion.1
  183.1 2.5 psum.15
  186.1 2.4 collective-permute-start.1
  188.6 14.3 %collective-permute-done.1 = bf16[3,2048]{0,1:T(8,128)(2,1)S(1)} collective-permute-done((bf16[3,2048]{0,1:T(8,128)(2,1)S(1)}, bf16[3,2048]{0,1:T(8,128)(2,1)S(1)}, u32[]{:S(2)}, u32[]{:S(2)}) %collective-permute-start.1) | collective-permute-done | bytes 12320 | tf_op jit(solution)/shard_map/ppermute | solution.py:17
  203.7 4.3 %multiply_convert_fusion.14 = bf16[256,2048]{0,1:T(8,128)(2,1)S(1)} fusion(bf16[256,2048]{0,1:T(8,128)(2,1)S(1)} %fusion.64, bf16[3,2048]{0,1:T(8,128)(2,1)} %copy-done.2, f32[2048]{0:T(1024)S(1)} %bitcast.327, f32[2048]{0:T(1024)S(1)} %bitcast.328, f32[2048]{0:T(1024)S(1)} %bitcast.329, f32[2048]{0:T(1024)S(1)} %bitcast.326), kind=kLoop, calls=%fused_computation.108 | loop fusion | flops 13107200 | bytes 2142208 | tf_op jit(solution)/shard_map/convert_element_type | solution.py:81
  209.7 8.5 %while.57 = (s32[]{:T(128)}, f32[2,256,16]{1,2,0:T(8,128)S(1)}, f32[2,256,16,64]{1,3,2,0:T(8,128)}, f32[2,16,64,64]{3,2,1,0:T(8,128)S(1)}, f32[2,256,16]{1,2,0:T...) while((s32[]{:T(128)}, f32[2,256,16]{1,2,0:T(8,128)S(1)}, ...), condition=%wide.region_14.15_spmd, body=%wide.region_11.14_spmd.sunk | while | flops 183844912 | bytes 3676037 | solution.py:93
  210.9 2.4 fusion.123
  215.1 2.4 fusion.123
  219.5 14.3 %all-gather.1 = f32[8,1,32]{2,1,0:T(1,128)S(1)} all-gather(f32[1,1,32]{2,1,0:T(1,128)S(1)} %reshape.224), channel_id=1, replica_groups=mesh['groups'=2,'seq'=8,'section'=2] {'seq'}, dimensions={0}, use_global_device_ids=true | all-gather | bytes 1152 | tf_op jit(solution)/shard_map/all_gather | solution.py:22
  233.8 108.8 %all-gather.7.cloned.1.call-done = f32[8,32,64,64]{3,2,1,0:T(8,128)} async-done(((f32[1,32,64,64]{3,2,1,0:T(8,128)}), f32[8,32,64,64]{3,2,1,0:T(8,128)}) %all-gather.7.cloned.1.call-update) | async-done | bytes 4194320 | tf_op jit(solution)/shard_map/all_gather | solution.py:22
  342.6 10.5 %while.59 = (s32[]{:T(128)}, f32[32,64,64]{2,1,0:T(8,128)S(1)}, s32[]{:T(128)}, f32[8,32]{1,0:T(8,128)S(1)}, f32[8,32,64,64]{3,2,1,0:T(8,128)}, /*index=5*/s32[]{:T(128)}, s32[]{:T(128)}) while((s32[]{:T(128)}, f32[32,64,64]{2,1,0:T(8,128)S(1)}, s32[]{:T(128)}, f32[8,32]{1,0:T(8,128)S(1)}, f32[8,32,64,64]{3,2,1,0:T(8,128)}, ...), condition=%wide.region_16.17_spmd.clone, body=%wide.region_15.16_spmd.clone.sunk | while | flops 524292 | bytes 1573353 | solution.py:31
  353.2 2.9 multiply_reduce_fusion
  358.2 3.9 %copy.55 = bf16[2,256,2048]{2,1,0:T(8,128)(2,1)} copy(bf16[2,256,2048]{1,2,0:T(8,128)(2,1)} %pad_maximum_fusion) | data formatting | bytes 4194304 | tf_op jit(solution)/shard_map/stack | solution.py:114
  (153 shorter events, 46.2 us)
Async XLA Ops:
  6.5 4.3 %copy-start.9 = (f32[2,2048]{1,0:T(2,128)S(1)}, f32[2,2048]{1,0:T(2,128)}, u32[]{:S(2)}) copy-start(f32[2,2048]{1,0:T(2,128)} %param.16) | copy-start | bytes 49156
  6.5 162.3 %all-gather.5.cloned.1.call-start = ((), (), s32[]{:S(2)}) async-start(), calls=%async_computation | async-start | bytes 9437184 | tf_op jit(solution)/shard_map/all_gather | solution.py:22
  8.0 6.8 %copy-start.5 = (bf16[2,4,2048]{2,1,0:T(4,128)(2,1)S(1)}, bf16[2,4,2048]{2,1,0:T(4,128)(2,1)}, u32[]{:S(2)}) copy-start(bf16[2,4,2048]{2,1,0:T(4,128)(2,1)} %param.17) | copy-start | bytes 98308
  8.0 6.8 %copy-start.3 = (bf16[2,256,2,128]{3,2,1,0:T(2,128)(2,1)S(1)}, bf16[2,256,2,128]{3,2,1,0:T(2,128)(2,1)}, u32[]{:S(2)}) copy-start(bf16[2,256,2,128]{3,2,1,0:T(2,128)(2,1)} %param.21) | copy-start | bytes 786436
  10.9 5.7 %copy-start.10 = (f32[2,32]{1,0:T(2,128)S(1)}, f32[2,32]{1,0:T(2,128)}, u32[]{:S(2)}) copy-start(f32[2,32]{1,0:T(2,128)} %param.18) | copy-start | bytes 772
  11.4 16.9 %collective-permute-start = (bf16[3,2048]{0,1:T(8,128)(2,1)S(1)}, bf16[3,2048]{0,1:T(8,128)(2,1)}, u32[]{:S(2)}, u32[]{:S(2)}) collective-permute-start(bf16[3,2048]{0,1:T(8,128)(2,1)S(1)} %slice.171), channel_id=1, source_target_pairs={{0,2},{2,4},{4,6},{6,8},{8,10},{10,12},{12,14},{1,3},{3,5},{5,7},{... | collective-permute-start | bytes 36872 | tf_op jit(solution)/shard_map/ppermute | solution.py:17
  34.9 10.9 %copy-start.11 = (f32[32]{0:T(128)S(1)}, f32[32]{0:T(128)}, u32[]{:S(2)}) copy-start(f32[32]{0:T(128)} %get-tuple-element.407) | copy-start | bytes 388
  44.5 1.1 copy-start
  45.6 297.0 %all-gather.7.cloned.1.call-start = ((), (), s32[]{:S(2)}) async-start(), calls=%async_computation.1 | async-start | bytes 9437184 | tf_op jit(solution)/shard_map/all_gather | solution.py:22
  183.0 5.5 %copy-start.4 = (f32[1,256,32]{1,2,0:T(8,128)S(1)}, f32[1,256,32]{1,2,0:T(8,128)}, u32[]{:S(2)}) copy-start(f32[1,256,32]{1,2,0:T(8,128)} %get-tuple-element.477) | copy-start | bytes 98308
  183.0 20.7 %copy-start.6 = (f32[1,1,2048]{2,1,0:T(1,128)S(1)}, f32[1,1,2048]{2,1,0:T(1,128)}, u32[]{:S(2)}) copy-start(f32[1,1,2048]{2,1,0:T(1,128)} %get-tuple-element.482) | copy-start | bytes 24580
  183.0 20.6 %copy-start.7 = (f32[1,1,2048]{2,1,0:T(1,128)S(1)}, f32[1,1,2048]{2,1,0:T(1,128)}, u32[]{:S(2)}) copy-start(f32[1,1,2048]{2,1,0:T(1,128)} %get-tuple-element.483) | copy-start | bytes 24580
  183.1 20.6 %copy-start.8 = (f32[1,1,2048]{2,1,0:T(1,128)S(1)}, f32[1,1,2048]{2,1,0:T(1,128)}, u32[]{:S(2)}) copy-start(f32[1,1,2048]{2,1,0:T(1,128)} %get-tuple-element.484) | copy-start | bytes 24580
  186.1 16.8 %collective-permute-start.1 = (bf16[3,2048]{0,1:T(8,128)(2,1)S(1)}, bf16[3,2048]{0,1:T(8,128)(2,1)S(1)}, u32[]{:S(2)}, u32[]{:S(2)}) collective-permute-start(bf16[3,2048]{0,1:T(8,128)(2,1)S(1)} %slice.183), channel_id=1, source_target_pairs={{0,2},{2,4},{4,6},{6,8},{8,10},{10,12},{12,14},{1,3},{3,5},{5,7},{... | collective-permute-start | bytes 36872 | tf_op jit(solution)/shard_map/ppermute | solution.py:17
  202.9 0.8 copy-start.2
  218.2 1.1 copy-start.1
Sparse Core Ops, SparseCore 0:
  45.7 123.0 all-gather.4
  219.4 123.1 all-gather.6
where the time goes:
time: 374 us; the launch traced here: 369 us
  waiting for transfers between devices  239 us (64%)
  other arithmetic  37.7 us (10%)
  blocking collectives  34.5 us (9%)
  local copies, waits for them, and re-layouts  20.6 us (6%)
  matrix products  17.6 us (5%)
  between operations  13.8 us (4%)
  starting transfers between devices  5.83 us (2%)
    all_gather x2, waiting for transfers between devices, carried_in(): pieces = jax.tree.map(lambda part: lax.all_gather(part, axis), value)  214 us
    all_gather x2, blocking collectives, carried_in(): pieces = jax.tree.map(lambda part: lax.all_gather(part, axis), value)  29.6 us
    ppermute x2, waiting for transfers between devices, from_behind(): return lax.ppermute(block, axis, route)  24.6 us
    select_n x14, other arithmetic, hop(): jnp.where(position < mine, new, old)  20.5 us
    dot_general x4, matrix products, group_terms(): jnp.einsum('hts,shp->thp', weights, mixed_g, preferred_element_type=jnp.f...  9.75 us
    convert_element_type x2, other arithmetic, local(): mixed = jax.nn.silu(total).astype(jnp.bfloat16)  8.58 us
  transfers between devices with their start and end apart: 4, of which 4 were waited for; matrix products, arithmetic and copies ran while one was open for 2% of the time, Pallas kernels for 0%

commit v1 on v0

v1 whole, which is shorter than its diff:
```python
import functools

import jax
import jax.numpy as jnp
from jax import lax
from jax.experimental import pallas as pl
from jax.experimental.pallas import tpu as pltpu
from jax.sharding import PartitionSpec as P

STATE = 64
WIDE = 256
EPSILON = 1e-05
LOG2E = 1.4426950408889634
MESH = pl.DeviceIdType.MESH
F32 = jnp.float32
BF16 = jnp.bfloat16


def split3(value):
    high = value.astype(BF16)
    rest = value - high.astype(F32)
    middle = rest.astype(BF16)
    low = (rest - middle.astype(F32)).astype(BF16)
    return high, middle, low


def kernel(
    n, sections, prompt, gain_in, conv_w, a_log, gain_out, dt, proj, out,
    r_split, f_split, r_exp, f_exp, q_rows, scores, b_t, c_two,
    pad, mixed, intra, local, squares, scale, scale_halo,
    d_own, d_pair, sum_in, rows_out, rows_in, part_out, part_in,
    z_out, z_in, x_out, x_in,
    d_sem, sum_sem, rows_sem, part_sem, z_send, z_recv, x_send, x_recv,
):
    layers, length, heads = dt.shape
    width = prompt.shape[1]
    head_dim = width // heads
    chunks = width // WIDE
    per_chunk = WIDE // head_dim
    groups = proj.shape[2] // (2 * STATE)
    per_group = chunks // groups
    taps = conv_w.shape[1]

    i = lax.axis_index("seq")
    s = lax.axis_index("section")
    pair = i + 1 - 2 * lax.rem(i, 2)
    first = lax.rem(i, 2) == 0
    has_before = i >= 1
    has_after = i < n - 1
    has_z_in = i >= 2
    has_z_out = i < n - 2

    def cols(c):
        return pl.ds(pl.multiple_of(c * WIDE, WIDE), WIDE)

    barrier = pltpu.get_barrier_semaphore()

    def greet(where):
        pl.semaphore_signal(barrier, inc=1, device_id=where, device_id_type=MESH)

    greet({"section": 1 - s})

    @pl.when(has_before)
    def _():
        greet({"seq": i - 1})
        greet({"seq": i - 1, "section": 1 - s})

    @pl.when(has_after)
    def _():
        greet({"seq": i + 1})
        greet({"seq": i + 1, "section": 1 - s})

    @pl.when(has_z_in)
    def _():
        greet({"seq": i - 2})

    @pl.when(has_z_out)
    def _():
        greet({"seq": i + 2})

    def remote(src, dst, send, recv, where):
        return pltpu.make_async_remote_copy(
            src_ref=src, dst_ref=dst, send_sem=send, recv_sem=recv,
            device_id=where, device_id_type=MESH,
        )

    def decay_copy():
        return remote(d_own, d_pair, d_sem.at[0], d_sem.at[1], {"seq": pair})

    def sum_copy(l):
        return remote(
            squares.at[l], sum_in.at[l], sum_sem.at[l, 0], sum_sem.at[l, 1], {"section": 1 - s}
        )

    def rows_copy(l):
        return remote(
            rows_out.at[l], rows_in.at[l], rows_sem.at[l, 0], rows_sem.at[l, 1], {"seq": i + 1}
        )

    def part_copy(l):
        return remote(
            part_out.at[l], part_in.at[l], part_sem.at[l, 0], part_sem.at[l, 1],
            {"seq": i + 1, "section": 1 - s},
        )

    def z_copy(l, c):
        return remote(
            z_out.at[l, c], z_in.at[l, c], z_send.at[l, c], z_recv.at[l, c], {"seq": i + 2}
        )

    def x_copy(l, c):
        return remote(
            x_out.at[l, c], x_in.at[l, c], x_send.at[l, c], x_recv.at[l, c], {"seq": pair}
        )

    def send_sums(l):
        part_out[l] = squares[l, length - 8 :, :]
        sum_copy(l).start()

        @pl.when(has_after)
        def _():
            rows_copy(l).start()
            part_copy(l).start()

    def fold(value):
        total = value[:, :128]
        for k in range(1, value.shape[1] // 128):
            total = total + value[:, k * 128 : (k + 1) * 128]
        return total

    squares[0] = jnp.zeros(squares.shape[1:], F32)

    @pl.loop(0, chunks)
    def _(c):
        h = prompt[:, cols(c)].astype(F32)
        squares[0] += fold(h * h)
        rows_out[0, :, cols(c)] = prompt[length - 16 :, cols(c)]

    @pl.when(i == 0)
    def _():
        rows_in[...] = jnp.zeros(rows_in.shape, BF16)
        part_in[...] = jnp.zeros(part_in.shape, F32)

    @pl.when(i < 2)
    def _():
        z_in[...] = jnp.zeros(z_in.shape, BF16)

    one = jnp.int32(1)
    zero = jnp.int32(0)
    expected = (
        1
        + 2 * jnp.where(has_before, one, zero)
        + 2 * jnp.where(has_after, one, zero)
        + jnp.where(has_z_in, one, zero)
        + jnp.where(has_z_out, one, zero)
    )
    pl.semaphore_wait(barrier, expected)
    send_sums(0)

    def wide(pieces):
        lanes = sum(p.shape[1] for p in pieces)
        rest = jnp.zeros((pieces[0].shape[0], 128 - lanes), pieces[0].dtype)
        return jnp.concatenate(pieces + [rest], axis=1)

    raw = wide([dt[l] for l in range(layers)])
    rate = jnp.exp(wide([a_log[l : l + 1, :] for l in range(layers)])) * LOG2E
    delta = jnp.maximum(raw, 0.0) + jnp.log(1.0 + jnp.exp(-jnp.abs(raw)))
    step = -delta * rate
    t_of = lax.broadcasted_iota(jnp.int32, (length, length), 0)
    s_of = lax.broadcasted_iota(jnp.int32, (length, length), 1)
    lower = t_of >= s_of
    running = jnp.dot(
        lower.astype(F32), step, preferred_element_type=F32, precision=lax.Precision.HIGHEST
    )
    behind = running - jnp.log(delta) * LOG2E
    ahead = running[length - 1 :, :] - behind
    turned = behind.T
    for lc in range(layers * chunks):
        q_rows[lc, :per_chunk, :] = turned[lc * per_chunk : (lc + 1) * per_chunk, :]
    for l in range(layers):
        mine = slice(l * heads, (l + 1) * heads)
        r_split[l] = wide([p.astype(F32) for p in split3(running[:, mine])]).astype(BF16)
        f_split[l] = wide([p.astype(F32) for p in split3(ahead[:, mine])]).astype(BF16)

    @pl.loop(0, layers * chunks)
    def _(lc):
        l = lc // chunks
        c = lax.rem(lc, chunks)
        row = lax.broadcasted_iota(jnp.int32, (128, WIDE), 0)
        lane = lax.broadcasted_iota(jnp.int32, (128, WIDE), 1)
        hit = (lax.rem(row, heads) == c * per_chunk + lane // head_dim) & (row < 3 * heads)
        pick = hit.astype(F32).astype(BF16)
        spread = jnp.dot(r_split[l], pick, preferred_element_type=F32)
        r_exp[lc] = spread
        d_own[pl.ds(lc, 1), :] = jnp.exp2(spread[length - 1 :, :])
        f_exp[lc] = jnp.exp2(jnp.dot(f_split[l], pick, preferred_element_type=F32))

    decay_copy().start()

    for l in range(layers):
        half = groups * STATE
        b_all = proj[l, :, :half].astype(F32)
        c_all = proj[l, :, half:].astype(F32)
        turned_b = b_all.T.astype(BF16)
        b_t[l] = turned_b
        for g in range(groups):
            c_g = c_all[:, g * STATE : (g + 1) * STATE]
            c_two[l * groups + g] = jnp.concatenate([c_g, c_g], axis=1).astype(BF16)
            both = jnp.dot(
                c_g.astype(BF16), turned_b[g * STATE : (g + 1) * STATE], preferred_element_type=F32
            )
            scores[l * groups + g] = jnp.where(lower, both, 0.0)

    head_of = lax.broadcasted_iota(jnp.int32, (length, WIDE), 1) // head_dim

    for l in range(layers):
        sum_copy(l).wait_recv()
        total = jnp.sum(squares[l] + sum_in[l], axis=1, keepdims=True)
        scale[...] = jnp.broadcast_to(
            lax.rsqrt(total / (width * sections) + EPSILON), scale.shape
        )

        @pl.when(has_before)
        def _():
            rows_copy(l).wait_recv()
            part_copy(l).wait_recv()

        halo_sum = part_in[l]
        for c in range(chunks):
            h = rows_in[l, :, c * WIDE : (c + 1) * WIDE].astype(F32)[8:]
            halo_sum = halo_sum + fold(h * h)
        halo_total = jnp.sum(halo_sum, axis=1, keepdims=True)
        scale_halo[...] = jnp.broadcast_to(
            lax.rsqrt(halo_total / (width * sections) + EPSILON), scale_halo.shape
        )
        if l == 0:
            decay_copy().wait_recv()

        def source(c):
            return prompt[:, cols(c)] if l == 0 else out[l - 1, :, cols(c)]

        def double(value):
            return jnp.concatenate([value] * (WIDE // 128), axis=1)

        def coefficients(c):
            own = d_own[pl.ds(l * chunks + c, 1), :]
            other = d_pair[pl.ds(l * chunks + c, 1), :]
            return own, other

        @pl.loop(0, chunks)
        def _(c):
            gain = gain_in[l : l + 1, cols(c)]
            h = source(c).astype(F32)
            normed = (h * double(scale[...]) * gain).astype(BF16).astype(F32)
            before = rows_in[l, :, cols(c)].astype(F32)[8:]
            pad[:8, :] = (before * double(scale_halo[...]) * gain).astype(BF16).astype(F32)
            pad[8:, :] = normed
            weight = conv_w[l, :, cols(c)].astype(F32)
            total = weight[taps - 1 : taps, :] * normed
            for k in range(taps - 1):
                start = 8 - (taps - 1) + k
                total = total + weight[k : k + 1, :] * pad[start : start + length, :]
            half = 0.5 * total
            here = (half + half * jnp.tanh(half)).astype(BF16)
            mixed[c] = here
            scaled = (f_exp[l * chunks + c] * here.astype(F32)).astype(BF16)
            g = c // per_group
            rows = pl.ds(pl.multiple_of(g * STATE, STATE), STATE)
            state = jnp.dot(b_t[l, rows, :], scaled, preferred_element_type=F32)
            local[c] = state
            own, other = coefficients(c)

            @pl.when(i < 2)
            def _():
                z_out[l, c] = (jnp.where(first, other, 1.0) * state).astype(BF16)

                @pl.when(has_z_out)
                def _():
                    z_copy(l, c).start()

        if l + 1 < layers:
            squares[l + 1] = jnp.zeros(squares.shape[1:], F32)

        def finish(c):
            x_copy(l, c).wait_recv()
            own, other = coefficients(c)
            g = l * groups + c // per_group
            entering = jnp.where(first, 1.0, other) * z_in[l, c].astype(F32) + x_in[l, c].astype(F32)
            high = entering.astype(BF16)
            low = (entering - high.astype(F32)).astype(BF16)
            inter = jnp.dot(
                c_two[g], jnp.concatenate([high, low], axis=0), preferred_element_type=F32
            )
            y = intra[c] + jnp.exp2(r_exp[l * chunks + c]) * inter
            row = lax.broadcasted_iota(jnp.int32, (WIDE, WIDE), 0) // head_dim
            same = (row == lax.broadcasted_iota(jnp.int32, (WIDE, WIDE), 1) // head_dim)
            power = jnp.dot(
                (y * y).astype(BF16), same.astype(F32).astype(BF16), preferred_element_type=F32
            )
            scaled = y * lax.rsqrt(power * (1.0 / head_dim) + EPSILON)
            after = (source(c).astype(F32) + scaled * gain_out[l : l + 1, cols(c)]).astype(BF16)
            out[l, :, cols(c)] = after
            if l + 1 < layers:
                rows_out[l + 1, :, cols(c)] = after[length - 16 :, :]
                wide_after = after.astype(F32)
                squares[l + 1] += fold(wide_after * wide_after)

        @pl.loop(0, chunks)
        def _(c):
            lc = l * chunks + c
            g = l * groups + c // per_group
            here = mixed[c]
            left, right = [], []
            for h in range(per_chunk):
                column = r_exp[lc, :, h * head_dim : h * head_dim + 1]
                decay = jnp.exp2(column - q_rows[lc, h : h + 1, :])
                left.append((decay * scores[g]).astype(BF16))
                right.append(jnp.where(head_of == h, here, jnp.zeros_like(here)))
            intra[c] = jnp.dot(
                jnp.concatenate(left, axis=1),
                jnp.concatenate(right, axis=0),
                preferred_element_type=F32,
            )
            own, other = coefficients(c)
            state = local[c]

            @pl.when(has_z_in)
            def _():
                z_copy(l, c).wait_recv()

                @pl.when(has_z_out)
                def _():
                    z_out[l, c] = (
                        own * other * z_in[l, c].astype(F32) + jnp.where(first, other, 1.0) * state
                    ).astype(BF16)
                    z_copy(l, c).start()

            arrived = z_in[l, c].astype(F32)
            x_out[l, c] = jnp.where(first, own * arrived + state, arrived).astype(BF16)
            x_copy(l, c).start()

            @pl.when(c >= 1)
            def _():
                finish(c - 1)

        finish(jnp.int32(chunks - 1))
        if l + 1 < layers:
            send_sums(l + 1)

    decay_copy().wait_send()
    for l in range(layers):
        sum_copy(l).wait_send()

        @pl.when(has_after)
        def _():
            rows_copy(l).wait_send()
            part_copy(l).wait_send()

        @pl.loop(0, chunks)
        def _(c):
            x_copy(l, c).wait_send()

            @pl.when(has_z_out)
            def _():
                z_copy(l, c).wait_send()


def local_part(n, sections, prompt, in_gain, conv_w, a_log, out_gain, dt_raw, proj):
    length, width = prompt.shape
    layers, _, heads = dt_raw.shape
    lanes = proj.shape[2] * proj.shape[3]
    chunks = width // WIDE
    groups = proj.shape[3] // STATE
    vmem = pltpu.VMEM
    dma = pltpu.SemaphoreType.DMA
    lc = layers * chunks
    scratch = [
        vmem((layers, length, 128), BF16),
        vmem((layers, length, 128), BF16),
        vmem((lc, length, WIDE), F32),
        vmem((lc, length, WIDE), F32),
        vmem((lc, 8, length), F32),
        vmem((layers * groups, length, length), F32),
        vmem((layers, groups * STATE, length), BF16),
        vmem((layers * groups, length, 2 * STATE), BF16),
        vmem((length + 8, WIDE), F32),
        vmem((chunks, length, WIDE), BF16),
        vmem((chunks, length, WIDE), F32),
        vmem((chunks, STATE, WIDE), F32),
        vmem((layers, length, 128), F32),
        vmem((length, 128), F32),
        vmem((8, 128), F32),
        vmem((lc, WIDE), F32),
        vmem((lc, WIDE), F32),
        vmem((layers, length, 128), F32),
        vmem((layers, 16, width), BF16),
        vmem((layers, 16, width), BF16),
        vmem((layers, 8, 128), F32),
        vmem((layers, 8, 128), F32),
        vmem((layers, chunks, STATE, WIDE), BF16),
        vmem((layers, chunks, STATE, WIDE), BF16),
        vmem((layers, chunks, STATE, WIDE), BF16),
        vmem((layers, chunks, STATE, WIDE), BF16),
        dma((2,)),
        dma((layers, 2)),
        dma((layers, 2)),
        dma((layers, 2)),
        dma((layers, chunks)),
        dma((layers, chunks)),
        dma((layers, chunks)),
        dma((layers, chunks)),
    ]
    return pl.pallas_call(
        functools.partial(kernel, n, sections),
        out_shape=jax.ShapeDtypeStruct((layers, length, width), BF16),
        in_specs=[pl.BlockSpec(memory_space=pltpu.VMEM)] * 7,
        out_specs=pl.BlockSpec(memory_space=pltpu.VMEM),
        scratch_shapes=scratch,
        compiler_params=pltpu.CompilerParams(
            collective_id=0, has_side_effects=True, vmem_limit_bytes=48 * 1024 * 1024
        ),
    )(prompt, in_gain, conv_w, a_log, out_gain, dt_raw, proj.reshape(layers, length, lanes))


def solution(mesh):
    in_specs = (
        P(("groups", "seq"), "section"),
        P(None, "section"),
        P(None, None, "section"),
        P(None, "section"),
        P(None, "section"),
        P(None, ("groups", "seq"), "section"),
        P(None, ("groups", "seq"), None, "section"),
    )
    out_specs = P(None, ("groups", "seq"), "section")
    part = functools.partial(local_part, mesh.shape["seq"], mesh.shape["section"])
    return jax.shard_map(part, mesh=mesh, in_specs=in_specs, out_specs=out_specs, check_vma=False)
```

time: 374 us -> 63.7 us (0.17)
  the two profiles are of different devices: /device:TPU:24 before, /device:TPU:26 now
where the time goes in v1:
time: 63.7 us; the launch traced here: 63.2 us
  Pallas kernels  55.7 us (87%)
  local copies, waits for them, and re-layouts  7.49 us (12%)
    pallas_call x1, Pallas kernels, local_part(): pl.pallas_call(functools.partial(kernel, n, sections), out_shape=jax.Shap...  55.7 us
    unnamed x12, local copies, waits for them, and re-layouts  6.37 us

profile of v1, /device:TPU:26, one launch (start us, length us, event | category | flops | bytes accessed | tf_op | source)
XLA Modules:
  0.0 63.2 jit_solution(7485808090460878033)
XLA Ops:
  0.0 1.0 %copy.8.dt = f32[2,256,32]{2,1,0:T(8,128)S(1)} copy(f32[2,256,32]{1,2,0:T(8,128)} %param.12) | data formatting | bytes 131072 | tf_op args[5]
  1.0 1.1 %reshape.3.proj = bf16[2,256,256]{2,1,0:T(8,128)(2,1)S(1)} reshape(bf16[2,256,2,128]{3,2,1,0:T(2,128)(2,1)} %param.13) | data formatting | bytes 524288 | tf_op jit(solution)/shard_map/reshape | solution.py:422
  2.1 0.0 copy-start
  2.1 1.2 %copy-done = bf16[256,2048]{1,0:T(8,128)(2,1)S(1)} copy-done((bf16[256,2048]{1,0:T(8,128)(2,1)S(1)}, bf16[256,2048]{1,0:T(8,128)(2,1)}, u32[]{:S(2)}) %copy-start) | copy-done | bytes 1048600
  3.3 0.0 copy-start.1
  3.3 0.8 %copy-done.1 = bf16[2,4,2048]{2,1,0:T(4,128)(2,1)S(1)} copy-done((bf16[2,4,2048]{2,1,0:T(4,128)(2,1)S(1)}, bf16[2,4,2048]{2,1,0:T(4,128)(2,1)}, u32[]{:S(2)}) %copy-start.1) | copy-done | bytes 32792
  4.1 0.0 copy-start.2
  4.1 0.7 %copy-done.2 = f32[2,2048]{1,0:T(2,128)S(1)} copy-done((f32[2,2048]{1,0:T(2,128)S(1)}, f32[2,2048]{1,0:T(2,128)}, u32[]{:S(2)}) %copy-start.2) | copy-done | bytes 16408
  4.8 0.0 copy-start.3
  4.8 0.7 %copy-done.3 = f32[2,2048]{1,0:T(2,128)S(1)} copy-done((f32[2,2048]{1,0:T(2,128)S(1)}, f32[2,2048]{1,0:T(2,128)}, u32[]{:S(2)}) %copy-start.3) | copy-done | bytes 16408
  5.5 0.0 copy-start.4
  5.5 0.7 %copy-done.4 = f32[2,32]{1,0:T(2,128)S(1)} copy-done((f32[2,32]{1,0:T(2,128)S(1)}, f32[2,32]{1,0:T(2,128)}, u32[]{:S(2)}) %copy-start.4) | copy-done | bytes 280
  6.2 55.7 %shard_map.73 = bf16[2,256,2048]{2,1,0:T(8,128)(2,1)S(1)} custom-call(bf16[256,2048]{1,0:T(8,128)(2,1)S(1)} %copy-done, f32[2,2048]{1,0:T(2,128)S(1)} %copy-done.2, bf16[2,4,2048]{2,1,0:T(4,128)(2,1)S(1)} %copy-done.1, f32[2,32]{1,0:T(2,128)S(1)} %copy-done.4, f32[2,2048]{1,0:T(2,128)S(1)} %copy-done.3, f32[2,256,32]{2,1,0:T(8,128)S(1)} %copy.8.dt, ...), custom_call_target="tpu_custom_call" | custom-call | tf_op jit(solution)/shard_map/pallas_call | solution.py:413
  61.9 1.3 %copy.10 = bf16[2,256,2048]{2,1,0:T(8,128)(2,1)} copy(bf16[2,256,2048]{2,1,0:T(8,128)(2,1)S(1)} %shard_map.73) | data formatting | bytes 4194304
Async XLA Ops:
  2.1 1.2 %copy-start = (bf16[256,2048]{1,0:T(8,128)(2,1)S(1)}, bf16[256,2048]{1,0:T(8,128)(2,1)}, u32[]{:S(2)}) copy-start(bf16[256,2048]{1,0:T(8,128)(2,1)} %prompt.1) | copy-start | bytes 3145732
  3.3 0.8 %copy-start.1 = (bf16[2,4,2048]{2,1,0:T(4,128)(2,1)S(1)}, bf16[2,4,2048]{2,1,0:T(4,128)(2,1)}, u32[]{:S(2)}) copy-start(bf16[2,4,2048]{2,1,0:T(4,128)(2,1)} %conv_w.1) | copy-start | bytes 98308
  4.1 0.7 %copy-start.2 = (f32[2,2048]{1,0:T(2,128)S(1)}, f32[2,2048]{1,0:T(2,128)}, u32[]{:S(2)}) copy-start(f32[2,2048]{1,0:T(2,128)} %gain_in.1) | copy-start | bytes 49156
  4.8 0.7 %copy-start.3 = (f32[2,2048]{1,0:T(2,128)S(1)}, f32[2,2048]{1,0:T(2,128)}, u32[]{:S(2)}) copy-start(f32[2,2048]{1,0:T(2,128)} %gain_out.1) | copy-start | bytes 49156
  5.5 0.7 %copy-start.4 = (f32[2,32]{1,0:T(2,128)S(1)}, f32[2,32]{1,0:T(2,128)}, u32[]{:S(2)}) copy-start(f32[2,32]{1,0:T(2,128)} %a_log.1) | copy-start | bytes 772

commit v2 on v1

--- a/solution.py
+++ b/solution.py
@@ -25,19 +25,20 @@
 
 
 def kernel(
-    n, sections, prompt, gain_in, conv_w, a_log, gain_out, dt, proj, out,
+    n, sections, prompt_h, gain_in_h, conv_w_h, a_log_h, gain_out_h, dt_h, proj_h, out,
+    prompt, gain_in, conv_w, a_log, gain_out, dt, proj, proj_wide, in_sem,
     r_split, f_split, r_exp, f_exp, q_rows, scores, b_t, c_two,
     pad, mixed, intra, local, squares, scale, scale_halo,
     d_own, d_pair, sum_in, rows_out, rows_in, part_out, part_in,
     z_out, z_in, x_out, x_in,
     d_sem, sum_sem, rows_sem, part_sem, z_send, z_recv, x_send, x_recv,
 ):
-    layers, length, heads = dt.shape
+    layers, heads, length = dt.shape
     width = prompt.shape[1]
     head_dim = width // heads
     chunks = width // WIDE
     per_chunk = WIDE // head_dim
-    groups = proj.shape[2] // (2 * STATE)
+    groups = proj.shape[2] // STATE
     per_group = chunks // groups
     taps = conv_w.shape[1]
 
@@ -53,6 +54,16 @@
     def cols(c):
         return pl.ds(pl.multiple_of(c * WIDE, WIDE), WIDE)
 
+    arrivals = {}
+    for k, (there, here) in enumerate(
+        (
+            (prompt_h, prompt), (dt_h, dt), (a_log_h, a_log), (proj_h, proj),
+            (gain_in_h, gain_in), (conv_w_h, conv_w), (gain_out_h, gain_out),
+        )
+    ):
+        arrivals[k] = pltpu.make_async_copy(there, here, in_sem.at[k])
+        arrivals[k].start()
+
     barrier = pltpu.get_barrier_semaphore()
 
     def greet(where):
@@ -84,8 +95,8 @@
             device_id=where, device_id_type=MESH,
         )
 
-    def decay_copy():
-        return remote(d_own, d_pair, d_sem.at[0], d_sem.at[1], {"seq": pair})
+    def decay_copy(l):
+        return remote(d_own.at[l], d_pair.at[l], d_sem.at[l, 0], d_sem.at[l, 1], {"seq": pair})
 
     def sum_copy(l):
         return remote(
@@ -129,6 +140,7 @@
         return total
 
     squares[0] = jnp.zeros(squares.shape[1:], F32)
+    arrivals[0].wait()
 
     @pl.loop(0, chunks)
     def _(c):
@@ -157,12 +169,16 @@
     pl.semaphore_wait(barrier, expected)
     send_sums(0)
 
+    for k in range(1, len(arrivals)):
+        arrivals[k].wait()
+
     def wide(pieces):
         lanes = sum(p.shape[1] for p in pieces)
         rest = jnp.zeros((pieces[0].shape[0], 128 - lanes), pieces[0].dtype)
         return jnp.concatenate(pieces + [rest], axis=1)
 
-    raw = wide([dt[l] for l in range(layers)])
+    idle = jnp.zeros((128 - layers * heads, length), F32)
+    raw = jnp.concatenate([dt[l] for l in range(layers)] + [idle], axis=0).T
     rate = jnp.exp(wide([a_log[l : l + 1, :] for l in range(layers)])) * LOG2E
     delta = jnp.maximum(raw, 0.0) + jnp.log(1.0 + jnp.exp(-jnp.abs(raw)))
     step = -delta * rate
@@ -182,25 +198,27 @@
         r_split[l] = wide([p.astype(F32) for p in split3(running[:, mine])]).astype(BF16)
         f_split[l] = wide([p.astype(F32) for p in split3(ahead[:, mine])]).astype(BF16)
 
-    @pl.loop(0, layers * chunks)
-    def _(lc):
-        l = lc // chunks
-        c = lax.rem(lc, chunks)
+    def spread_steps(l, c):
+        lc = l * chunks + c
         row = lax.broadcasted_iota(jnp.int32, (128, WIDE), 0)
         lane = lax.broadcasted_iota(jnp.int32, (128, WIDE), 1)
         hit = (lax.rem(row, heads) == c * per_chunk + lane // head_dim) & (row < 3 * heads)
         pick = hit.astype(F32).astype(BF16)
         spread = jnp.dot(r_split[l], pick, preferred_element_type=F32)
         r_exp[lc] = spread
-        d_own[pl.ds(lc, 1), :] = jnp.exp2(spread[length - 1 :, :])
+        d_own[l, pl.ds(c, 1), :] = jnp.exp2(spread[length - 1 :, :])
         f_exp[lc] = jnp.exp2(jnp.dot(f_split[l], pick, preferred_element_type=F32))
 
-    decay_copy().start()
+    @pl.loop(0, chunks)
+    def _(c):
+        spread_steps(0, c)
+
+    decay_copy(0).start()
 
     for l in range(layers):
-        half = groups * STATE
-        b_all = proj[l, :, :half].astype(F32)
-        c_all = proj[l, :, half:].astype(F32)
+        proj_wide[...] = proj[l].astype(F32)
+        b_all = proj_wide[pl.ds(0, length, stride=2), :]
+        c_all = proj_wide[pl.ds(1, length, stride=2), :]
         turned_b = b_all.T.astype(BF16)
         b_t[l] = turned_b
         for g in range(groups):
@@ -233,8 +251,7 @@
         scale_halo[...] = jnp.broadcast_to(
             lax.rsqrt(halo_total / (width * sections) + EPSILON), scale_halo.shape
         )
-        if l == 0:
-            decay_copy().wait_recv()
+        decay_copy(l).wait_recv()
 
         def source(c):
             return prompt[:, cols(c)] if l == 0 else out[l - 1, :, cols(c)]
@@ -243,8 +260,8 @@
             return jnp.concatenate([value] * (WIDE // 128), axis=1)
 
         def coefficients(c):
-            own = d_own[pl.ds(l * chunks + c, 1), :]
-            other = d_pair[pl.ds(l * chunks + c, 1), :]
+            own = d_own[l, pl.ds(c, 1), :]
+            other = d_pair[l, pl.ds(c, 1), :]
             return own, other
 
         @pl.loop(0, chunks)
@@ -339,16 +356,21 @@
             x_out[l, c] = jnp.where(first, own * arrived + state, arrived).astype(BF16)
             x_copy(l, c).start()
 
-            @pl.when(c >= 1)
-            def _():
-                finish(c - 1)
-
-        finish(jnp.int32(chunks - 1))
+            if l + 1 < layers:
+                spread_steps(l + 1, c)
+
+        if l + 1 < layers:
+            decay_copy(l + 1).start()
+
+        @pl.loop(0, chunks)
+        def _(c):
+            finish(c)
+
         if l + 1 < layers:
             send_sums(l + 1)
 
-    decay_copy().wait_send()
     for l in range(layers):
+        decay_copy(l).wait_send()
         sum_copy(l).wait_send()
 
         @pl.when(has_after)
@@ -368,13 +390,18 @@
 def local_part(n, sections, prompt, in_gain, conv_w, a_log, out_gain, dt_raw, proj):
     length, width = prompt.shape
     layers, _, heads = dt_raw.shape
-    lanes = proj.shape[2] * proj.shape[3]
+    operands = (
+        prompt, in_gain, conv_w, a_log, out_gain,
+        dt_raw.transpose(0, 2, 1), proj.reshape(layers, 2 * length, proj.shape[3]),
+    )
     chunks = width // WIDE
     groups = proj.shape[3] // STATE
     vmem = pltpu.VMEM
     dma = pltpu.SemaphoreType.DMA
     lc = layers * chunks
-    scratch = [
+    scratch = [vmem(value.shape, value.dtype) for value in operands] + [
+        vmem((2 * length, proj.shape[3]), F32),
+        dma((len(operands),)),
         vmem((layers, length, 128), BF16),
         vmem((layers, length, 128), BF16),
         vmem((lc, length, WIDE), F32),
@@ -390,8 +417,8 @@
         vmem((layers, length, 128), F32),
         vmem((length, 128), F32),
         vmem((8, 128), F32),
-        vmem((lc, WIDE), F32),
-        vmem((lc, WIDE), F32),
+        vmem((layers, chunks, WIDE), F32),
+        vmem((layers, chunks, WIDE), F32),
         vmem((layers, length, 128), F32),
         vmem((layers, 16, width), BF16),
         vmem((layers, 16, width), BF16),
@@ -401,7 +428,7 @@
         vmem((layers, chunks, STATE, WIDE), BF16),
         vmem((layers, chunks, STATE, WIDE), BF16),
         vmem((layers, chunks, STATE, WIDE), BF16),
-        dma((2,)),
+        dma((layers, 2)),
         dma((layers, 2)),
         dma((layers, 2)),
         dma((layers, 2)),
@@ -413,13 +440,13 @@
     return pl.pallas_call(
         functools.partial(kernel, n, sections),
         out_shape=jax.ShapeDtypeStruct((layers, length, width), BF16),
-        in_specs=[pl.BlockSpec(memory_space=pltpu.VMEM)] * 7,
+        in_specs=[pl.BlockSpec(memory_space=pltpu.HBM)] * len(operands),
         out_specs=pl.BlockSpec(memory_space=pltpu.VMEM),
         scratch_shapes=scratch,
         compiler_params=pltpu.CompilerParams(
-            collective_id=0, has_side_effects=True, vmem_limit_bytes=48 * 1024 * 1024
+            collective_id=0, has_side_effects=True, vmem_limit_bytes=60 * 1024 * 1024
         ),
-    )(prompt, in_gain, conv_w, a_log, out_gain, dt_raw, proj.reshape(layers, length, lanes))
+    )(*operands)
 
 
 def solution(mesh):

time: 63.7 us -> 44.1 us (0.69)
  the two profiles are of different devices: /device:TPU:26 before, /device:TPU:24 now
where the time goes in v2:
time: 44.1 us; the launch traced here: 44 us
  Pallas kernels  40.8 us (93%)
  local copies, waits for them, and re-layouts  3.16 us (7%)
    pallas_call x1, Pallas kernels, local_part(): pl.pallas_call(functools.partial(kernel, n, sections), out_shape=jax.Shap...  40.8 us
    unnamed x1, local copies, waits for them, and re-layouts  3.16 us

profile of v2, /device:TPU:24, one launch (start us, length us, event | category | flops | bytes accessed | tf_op | source)
XLA Modules:
  0.0 44.0 jit_solution(6200663041222767976)
XLA Ops:
  0.0 40.8 %shard_map.73 = bf16[2,256,2048]{2,1,0:T(8,128)(2,1)} custom-call(bf16[256,2048]{1,0:T(8,128)(2,1)} %prompt_h.1, f32[2,2048]{1,0:T(2,128)} %gain_in_h.1, bf16[2,4,2048]{2,1,0:T(4,128)(2,1)} %conv_w_h.1, f32[2,32]{1,0:T(2,128)} %a_log_h.1, f32[2,2048]{1,0:T(2,128)} %gain_out_h.1, f32[2,32,256]{2,1,0:T(8,128)} %bitcast.3, bf16[2,512,128]{2,1,0:T(8,128)(2,1)} %bitcast.2), custom_call_target="tpu_custom_call" | custom-call | tf_op jit(solution)/shard_map/pallas_call | solution.py:440
  40.8 3.2 %copy.9 = bf16[2,256,2048]{2,1,0:T(8,128)(2,1)} copy(bf16[2,256,2048]{2,1,0:T(8,128)(2,1)} %shard_map.73) | data formatting | bytes 4194304

commit v3 on v2

--- a/solution.py
+++ b/solution.py
@@ -439,7 +439,7 @@
     ]
     return pl.pallas_call(
         functools.partial(kernel, n, sections),
-        out_shape=jax.ShapeDtypeStruct((layers, length, width), BF16),
+        out_shape=pltpu.VMEM((layers, length, width), BF16),
         in_specs=[pl.BlockSpec(memory_space=pltpu.HBM)] * len(operands),
         out_specs=pl.BlockSpec(memory_space=pltpu.VMEM),
         scratch_shapes=scratch,

time: 44.1 us -> 40.9 us (0.927)
  local copies, waits for them, and re-layouts: 3.16 us -> 1.32 us
  Pallas kernels: 40.8 us -> 39.4 us
    unnamed x1, local copies, waits for them, and re-layouts: 3.16 us -> 1.32 us
    pallas_call x1, Pallas kernels: 40.8 us -> 39.4 us  [local_part(): pl.pallas_call(functools.partial(kernel, n, sections), out_shape=pltpu.VM...]
where the time goes in v3:
time: 40.9 us; the launch traced here: 40.8 us
  Pallas kernels  39.4 us (96%)
  local copies, waits for them, and re-layouts  1.32 us (3%)
    pallas_call x1, Pallas kernels, local_part(): pl.pallas_call(functools.partial(kernel, n, sections), out_shape=pltpu.VM...  39.4 us
    unnamed x1, local copies, waits for them, and re-layouts  1.32 us

profile of v3, /device:TPU:24, one launch (start us, length us, event | category | flops | bytes accessed | tf_op | source)
XLA Modules:
  0.0 40.8 jit_solution(519602177232647442)
XLA Ops:
  0.0 39.4 %shard_map.73 = bf16[2,256,2048]{2,1,0:T(8,128)(2,1)S(1)} custom-call(bf16[256,2048]{1,0:T(8,128)(2,1)} %prompt_h.1, f32[2,2048]{1,0:T(2,128)} %gain_in_h.1, bf16[2,4,2048]{2,1,0:T(4,128)(2,1)} %conv_w_h.1, f32[2,32]{1,0:T(2,128)} %a_log_h.1, f32[2,2048]{1,0:T(2,128)} %gain_out_h.1, f32[2,32,256]{2,1,0:T(8,128)} %bitcast.3, bf16[2,512,128]{2,1,0:T(8,128)(2,1)} %bitcast.2), custom_call_target="tpu_custom_call" | custom-call | tf_op jit(solution)/shard_map/pallas_call | solution.py:440
  39.4 1.3 %copy.9 = bf16[2,256,2048]{2,1,0:T(8,128)(2,1)} copy(bf16[2,256,2048]{2,1,0:T(8,128)(2,1)S(1)} %shard_map.73) | data formatting | bytes 4194304

commit v4 on v3

--- a/solution.py
+++ b/solution.py
@@ -166,8 +166,6 @@
         + jnp.where(has_z_in, one, zero)
         + jnp.where(has_z_out, one, zero)
     )
-    pl.semaphore_wait(barrier, expected)
-    send_sums(0)
 
     for k in range(1, len(arrivals)):
         arrivals[k].wait()
@@ -208,6 +206,9 @@
         r_exp[lc] = spread
         d_own[l, pl.ds(c, 1), :] = jnp.exp2(spread[length - 1 :, :])
         f_exp[lc] = jnp.exp2(jnp.dot(f_split[l], pick, preferred_element_type=F32))
+
+    pl.semaphore_wait(barrier, expected)
+    send_sums(0)
 
     @pl.loop(0, chunks)
     def _(c):
@@ -324,6 +325,24 @@
 
         @pl.loop(0, chunks)
         def _(c):
+            own, other = coefficients(c)
+            state = local[c]
+
+            @pl.when(has_z_in)
+            def _():
+                z_copy(l, c).wait_recv()
+
+                @pl.when(has_z_out)
+                def _():
+                    z_out[l, c] = (
+                        own * other * z_in[l, c].astype(F32) + jnp.where(first, other, 1.0) * state
+                    ).astype(BF16)
+                    z_copy(l, c).start()
+
+            arrived = z_in[l, c].astype(F32)
+            x_out[l, c] = jnp.where(first, own * arrived + state, arrived).astype(BF16)
+            x_copy(l, c).start()
+
             lc = l * chunks + c
             g = l * groups + c // per_group
             here = mixed[c]
@@ -338,28 +357,12 @@
                 jnp.concatenate(right, axis=0),
                 preferred_element_type=F32,
             )
-            own, other = coefficients(c)
-            state = local[c]
-
-            @pl.when(has_z_in)
-            def _():
-                z_copy(l, c).wait_recv()
-
-                @pl.when(has_z_out)
-                def _():
-                    z_out[l, c] = (
-                        own * other * z_in[l, c].astype(F32) + jnp.where(first, other, 1.0) * state
-                    ).astype(BF16)
-                    z_copy(l, c).start()
-
-            arrived = z_in[l, c].astype(F32)
-            x_out[l, c] = jnp.where(first, own * arrived + state, arrived).astype(BF16)
-            x_copy(l, c).start()
-
-            if l + 1 < layers:
+
+        if l + 1 < layers:
+            @pl.loop(0, chunks)
+            def _(c):
                 spread_steps(l + 1, c)
 
-        if l + 1 < layers:
             decay_copy(l + 1).start()
 
         @pl.loop(0, chunks)

time: 40.9 us -> 40.6 us (level)
  no operation moved by 1% of the time
where the time goes in v4:
time: 40.6 us; the launch traced here: 40.5 us
  Pallas kernels  39.1 us (96%)
  local copies, waits for them, and re-layouts  1.32 us (3%)
    pallas_call x1, Pallas kernels, local_part(): pl.pallas_call(functools.partial(kernel, n, sections), out_shape=pltpu.VM...  39.1 us
    unnamed x1, local copies, waits for them, and re-layouts  1.32 us

profile of v4, /device:TPU:24, one launch (start us, length us, event | category | flops | bytes accessed | tf_op | source)
XLA Modules:
  0.0 40.5 jit_solution(13114479656794141513)
XLA Ops:
  0.0 39.1 %shard_map.73 = bf16[2,256,2048]{2,1,0:T(8,128)(2,1)S(1)} custom-call(bf16[256,2048]{1,0:T(8,128)(2,1)} %prompt_h.1, f32[2,2048]{1,0:T(2,128)} %gain_in_h.1, bf16[2,4,2048]{2,1,0:T(4,128)(2,1)} %conv_w_h.1, f32[2,32]{1,0:T(2,128)} %a_log_h.1, f32[2,2048]{1,0:T(2,128)} %gain_out_h.1, f32[2,32,256]{2,1,0:T(8,128)} %bitcast.3, bf16[2,512,128]{2,1,0:T(8,128)(2,1)} %bitcast.2), custom_call_target="tpu_custom_call" | custom-call | tf_op jit(solution)/shard_map/pallas_call | solution.py:443
  39.1 1.3 %copy.9 = bf16[2,256,2048]{2,1,0:T(8,128)(2,1)} copy(bf16[2,256,2048]{2,1,0:T(8,128)(2,1)S(1)} %shard_map.73) | data formatting | bytes 4194304
